TPU v7x, 32 devices: a whole 2x2x4 slice. The times are simulated.
32 devices in a mesh: groups: 2 (over x), row: 16 (over z, y, core).
Axes of the slice: x: 2, y: 2, z: 4, core: 2. Of those that a mesh axis runs over, the one named last changes fastest.
Arguments:
- a_blocks: float32 [16384, 2048], P(('groups', 'row')), parts along dimension 0, may hold values from -4 to 4
- a_mask: int32 [128, 16], P(('groups', 'row')), parts along dimension 0, may hold values 0 or 1
- b_panel: float32 [16384, 2048], P(('groups', 'row')), parts along dimension 0, may hold values from -4 to 4
- b_mask: int32 [128, 16], P(('groups', 'row')), parts along dimension 0, may hold values 0 or 1
Outputs:
- c_slab: float32 [16384, 2048], P(('groups', 'row')), parts along dimension 0
There are 2 independent parts, one for each index of `groups`. A program takes and returns all parts, laid end to end along the dimension named above; each array names one. Nothing has to cross between parts.
All inputs are finite; a program needn't handle non-finite values. No bound on the sum of `a_mask` or of `b_mask` on one device may be relied on, other than what follows from the above.
Results may differ from a plain program's by a relative error of at most 0.0001.
Values sent between devices are 32-bit elements; how exact they have to be, the bound alone decides.
A program may use at most 128 MiB of HBM per device.

v0:
```python
import jax
import jax.numpy as jnp
from jax import lax
from jax.sharding import PartitionSpec as P


def from_behind(value, axis, steps):
    count = lax.axis_size(axis)
    pairs = [(source, (source + steps) % count) for source in range(count)]
    return lax.ppermute(value, axis, pairs)


def shards(a_blocks, a_mask, b_panel, b_mask):
    rows = a_blocks.shape[0]
    row_blocks = a_mask.shape[0]
    block = rows // row_blocks
    inner_blocks = b_mask.shape[0]
    col_blocks = b_mask.shape[1]
    steps = a_mask.shape[1] // inner_blocks
    masked_a = (
        a_blocks.reshape(row_blocks, block, steps * inner_blocks, block)
        * a_mask.astype(jnp.float32)[:, None, :, None]
    ).reshape(rows, steps, inner_blocks * block)
    masked_b = (
        b_panel.reshape(inner_blocks, block, col_blocks, block)
        * b_mask.astype(jnp.float32)[:, None, :, None]
    ).reshape(inner_blocks * block, col_blocks * block)
    panels = [masked_b]
    current = masked_b
    for step in range(1, steps):
        current = from_behind(current, "row", 1)
        panels.append(current)
    total = jnp.zeros((rows, col_blocks * block), jnp.float32)
    for step in range(steps):
        total = total + jnp.dot(
            masked_a[:, step, :],
            panels[step],
            precision=lax.Precision.HIGHEST,
            preferred_element_type=jnp.float32,
        )
    return total


def solution(mesh):
    return jax.shard_map(
        shards,
        mesh=mesh,
        in_specs=(
            P(("groups", "row"), None),
            P(("groups", "row"), None),
            P(("groups", "row"), None),
            P(("groups", "row"), None),
        ),
        out_specs=P(("groups", "row"), None),
        check_vma=False,
    )
```

profile of v0, /device:TPU:0, one launch (start us, length us, event | category | flops | bytes accessed | tf_op | source)
XLA Modules:
  0.0 172.2 jit_solution(8701758458612912779)
XLA Ops:
  0.0 0.0 copy-start.2
  0.0 0.8 convert_element_type.7
  0.8 0.3 mul.25
  1.2 1.0 copy-done.2
  2.2 0.0 copy-start.5
  2.2 2.3 %bitcast_multiply_fusion = f32[512,2048]{1,0:T(8,128)S(1)} fusion(f32[512,2048]{1,0:T(8,128)S(1)} %copy-done.2, f32[64,8,16,128]{3,2,1,0:T(8,128)S(1)} %bitcast.22), kind=kLoop, calls=%fused_computation | loop fusion | flops 1048576 | bytes 12582912 | tf_op jit(solution)/shard_map/mul | solution.py:25
  4.5 0.0 copy-start
  4.5 2.0 %copy-done = f32[512,2048]{1,0:T(8,128)} copy-done((f32[512,2048]{1,0:T(8,128)}, f32[512,2048]{1,0:T(8,128)S(1)}, u32[]{:S(2)}) %copy-start) | copy-done | bytes 4194328
  6.5 0.5 collective-permute-start
  6.9 51.2 %collective-permute-done = f32[512,2048]{1,0:T(8,128)S(1)} collective-permute-done((f32[512,2048]{1,0:T(8,128)S(1)}, f32[512,2048]{1,0:T(8,128)S(1)}, u32[]{:S(2)}, u32[]{:S(2)}) %collective-permute-start) | collective-permute-done | bytes 4194336 | tf_op jit(solution)/shard_map/ppermute | solution.py:10
  58.1 0.0 copy-start.3
  58.1 2.0 %copy-done.3 = f32[512,2048]{1,0:T(8,128)} copy-done((f32[512,2048]{1,0:T(8,128)}, f32[512,2048]{1,0:T(8,128)S(1)}, u32[]{:S(2)}) %copy-start.3) | copy-done | bytes 4194328
  60.1 0.0 collective-permute-start.1
  60.1 50.7 %collective-permute-done.1 = f32[512,2048]{1,0:T(8,128)} collective-permute-done((f32[512,2048]{1,0:T(8,128)S(1)}, f32[512,2048]{1,0:T(8,128)}, u32[]{:S(2)}, u32[]{:S(2)}) %collective-permute-start.1) | collective-permute-done | bytes 4194336 | tf_op jit(solution)/shard_map/ppermute | solution.py:10
  110.8 0.0 collective-permute-start.2
  110.8 0.0 copy-done.5
  110.8 2.4 %mul.22 = f32[4,128,16,128]{3,2,1,0:T(8,128)} broadcast(f32[4,16]{1,0:T(4,128)S(1)} %convert_element_type.6), dimensions={0,2} | broadcast | bytes 4194560 | tf_op jit(solution)/shard_map/mul | solution.py:21
  113.2 5.2 %mul.23 = f32[512,4,512]{2,1,0:T(4,128)} reshape(f32[4,128,16,128]{3,2,1,0:T(8,128)} %mul.22) | data formatting | bytes 8388608 | tf_op jit(solution)/shard_map/mul | solution.py:21
  118.4 6.0 %reshape.11 = f32[512,4,512]{2,1,0:T(4,128)} reshape(f32[512,2048]{1,0:T(8,128)} %param.4) | data formatting | bytes 8388608 | tf_op jit(solution)/shard_map/reshape | solution.py:21
  124.4 4.5 %mul.24 = f32[512,4,512]{2,1,0:T(4,128)S(1)} multiply(f32[512,4,512]{2,1,0:T(4,128)} %reshape.11, f32[512,4,512]{2,1,0:T(4,128)} %mul.23) | non-fusion elementwise | flops 1048576 | bytes 12582912 | tf_op jit(solution)/shard_map/mul | solution.py:21
  129.0 0.0 copy-start.1
  129.0 3.3 %fusion.11 = (f32[512,1,512]{2,1,0:T(1,128)S(1)}, f32[512,1,512]{2,1,0:T(1,128)S(1)}, f32[512,1,512]{2,1,0:T(1,128)S(1)}, f32[512,1,512]{2,1,0:T(1,128)S(1)}) fusion(f32[512,4,512]{2,1,0:T(4,128)S(1)} %mul.24), kind=kLoop, calls=%fused_computation.13 | loop fusion | bytes 8388608 | tf_op jit(solution)/shard_map/slice | solution.py:36
  132.3 0.0 copy-done.1
  132.3 0.0 copy-start.4
  132.3 7.1 %fusion.8 = f32[512,2048]{1,0:T(8,128)S(1)} fusion(f32[512,2048]{1,0:T(8,128)S(1)} %copy-done.1, f32[512,1,512]{2,1,0:T(1,128)S(1)} %get-tuple-element.8), kind=kOutput, calls=%fused_computation.10 | convolution fusion | flops 6442450944 | bytes 9437184 | tf_op jit(solution)/shard_map/dot_general | solution.py:35
  139.4 0.0 copy-done.4
  139.4 7.3 %fusion.5 = f32[512,2048]{1,0:T(8,128)S(1)} fusion(f32[512,2048]{1,0:T(8,128)S(1)} %copy-done.4, f32[512,1,512]{2,1,0:T(1,128)S(1)} %get-tuple-element.7), kind=kOutput, calls=%fused_computation.7 | convolution fusion | flops 6442450944 | bytes 9437184 | tf_op jit(solution)/shard_map/dot_general | solution.py:35
  146.8 8.8 %fusion.2 = f32[512,2048]{1,0:T(8,128)S(1)} fusion(f32[512,2048]{1,0:T(8,128)} %collective-permute-done.1, f32[512,1,512]{2,1,0:T(1,128)S(1)} %get-tuple-element.6), kind=kOutput, calls=%fused_computation.4 | convolution fusion | flops 6442450944 | bytes 9437184 | tf_op jit(solution)/shard_map/dot_general | solution.py:35
  155.6 6.2 %collective-permute-done.2 = f32[512,2048]{1,0:T(8,128)} collective-permute-done((f32[512,2048]{1,0:T(8,128)}, f32[512,2048]{1,0:T(8,128)}, u32[]{:S(2)}, u32[]{:S(2)}) %collective-permute-start.2) | collective-permute-done | bytes 4194336 | tf_op jit(solution)/shard_map/ppermute | solution.py:10
  161.7 10.5 %add_add_fusion = f32[512,2048]{1,0:T(8,128)} fusion(f32[512,2048]{1,0:T(8,128)S(1)} %fusion.2, f32[512,2048]{1,0:T(8,128)S(1)} %fusion.8, f32[512,2048]{1,0:T(8,128)S(1)} %fusion.5, f32[512,2048]{1,0:T(8,128)} %collective-permute-done.2, f32[512,1,512]{2,1,0:T(1,128)S(1)} %get-tuple-element.5), kind=kOutput, calls=%fused_computation.1 | convolution fusion | flops 6445596672 | bytes 22020096 | tf_op jit(solution)/shard_map/dot_general | solution.py:35
  (1 shorter events, 0.0 us)
Async XLA Ops:
  0.0 2.2 %copy-start.2 = (f32[512,2048]{1,0:T(8,128)S(1)}, f32[512,2048]{1,0:T(8,128)}, u32[]{:S(2)}) copy-start(f32[512,2048]{1,0:T(8,128)} %param.6) | copy-start | bytes 12582916
  2.2 108.6 %copy-start.5 = (s32[4,16]{1,0:T(4,128)S(1)}, s32[4,16]{1,0:T(4,128)}, u32[]{:S(2)}) copy-start(s32[4,16]{1,0:T(4,128)} %param.5) | copy-start | bytes 772
  4.5 2.0 %copy-start = (f32[512,2048]{1,0:T(8,128)}, f32[512,2048]{1,0:T(8,128)S(1)}, u32[]{:S(2)}) copy-start(f32[512,2048]{1,0:T(8,128)S(1)} %bitcast_multiply_fusion) | copy-start | bytes 12582916
  6.5 51.6 %collective-permute-start = (f32[512,2048]{1,0:T(8,128)S(1)}, f32[512,2048]{1,0:T(8,128)S(1)}, u32[]{:S(2)}, u32[]{:S(2)}) collective-permute-start(f32[512,2048]{1,0:T(8,128)S(1)} %bitcast_multiply_fusion), channel_id=1, source_target_pairs={{0,1},{1,2},{2,3},{3,4},{4,5},{5,6},{6,7},{7,8},{8,9},{9,10},{10,1... | collective-permute-start | bytes 12582920 | tf_op jit(solution)/shard_map/ppermute | solution.py:10
  58.1 2.0 %copy-start.3 = (f32[512,2048]{1,0:T(8,128)}, f32[512,2048]{1,0:T(8,128)S(1)}, u32[]{:S(2)}) copy-start(f32[512,2048]{1,0:T(8,128)S(1)} %collective-permute-done) | copy-start | bytes 12582916
  60.1 50.7 %collective-permute-start.1 = (f32[512,2048]{1,0:T(8,128)S(1)}, f32[512,2048]{1,0:T(8,128)}, u32[]{:S(2)}, u32[]{:S(2)}) collective-permute-start(f32[512,2048]{1,0:T(8,128)S(1)} %collective-permute-done), channel_id=1, source_target_pairs={{0,1},{1,2},{2,3},{3,4},{4,5},{5,6},{6,7},{7,8},{8,9},{9,10},{10,1... | collective-permute-start | bytes 12582920 | tf_op jit(solution)/shard_map/ppermute | solution.py:10
  110.8 50.9 %collective-permute-start.2 = (f32[512,2048]{1,0:T(8,128)}, f32[512,2048]{1,0:T(8,128)}, u32[]{:S(2)}, u32[]{:S(2)}) collective-permute-start(f32[512,2048]{1,0:T(8,128)} %collective-permute-done.1), channel_id=1, source_target_pairs={{0,1},{1,2},{2,3},{3,4},{4,5},{5,6},{6,7},{7,8},{8,9},{9,10},{10,1... | collective-permute-start | bytes 12582920 | tf_op jit(solution)/shard_map/ppermute | solution.py:10
  129.0 3.3 %copy-start.1 = (f32[512,2048]{1,0:T(8,128)S(1)}, f32[512,2048]{1,0:T(8,128)}, u32[]{:S(2)}) copy-start(f32[512,2048]{1,0:T(8,128)} %copy-done) | copy-start | bytes 12582916
  132.3 7.1 %copy-start.4 = (f32[512,2048]{1,0:T(8,128)S(1)}, f32[512,2048]{1,0:T(8,128)}, u32[]{:S(2)}) copy-start(f32[512,2048]{1,0:T(8,128)} %copy-done.3) | copy-start | bytes 12582916
where the time goes:
time: 173 us; the launch traced here: 172 us
  waiting for transfers between devices  108 us (62%)
  matrix products  33.7 us (19%)
  local copies, waits for them, and re-layouts  22.2 us (13%)
  other arithmetic  7.65 us (4%)
    ppermute x3, waiting for transfers between devices, from_behind(): return lax.ppermute(value, axis, pairs)  108 us
    dot_general x4, matrix products, shards(): jnp.dot(masked_a[:, step, :], panels[step], precision=lax.Precision.HIGHE...  33.7 us
    mul x2, local copies, waits for them, and re-layouts, shards(): a_blocks.reshape(row_blocks, block, steps * inner_blocks, block)  7.6 us
    reshape x1, local copies, waits for them, and re-layouts, shards(): a_blocks.reshape(row_blocks, block, steps * inner_blocks, block)  6.01 us
    unnamed x12, local copies, waits for them, and re-layouts  4.98 us
    mul x1, other arithmetic, shards(): a_blocks.reshape(row_blocks, block, steps * inner_blocks, block)  4.55 us
  transfers between devices with their start and end apart: 3, of which 3 were waited for; matrix products, arithmetic and copies ran while one was open for 26% of the time, Pallas kernels for 0%

commit v1 on v0

v1 whole, which is shorter than its diff:
```python
import functools

import jax
import jax.numpy as jnp
from jax import lax
from jax.experimental import pallas as pl
from jax.experimental.pallas import tpu as pltpu
from jax.sharding import PartitionSpec as P

SLOTS = 16
PIECE = 4
TABLE = (8, 128)
AHEAD = 3
MIB = 1 << 20


def from_behind(value, axis, steps):
    count = lax.axis_size(axis)
    pairs = [(source, (source + steps) % count) for source in range(count)]
    return lax.ppermute(value, axis, pairs)


def dense(a_blocks, a_mask, b_panel, b_mask):
    rows = a_blocks.shape[0]
    row_blocks = a_mask.shape[0]
    block = rows // row_blocks
    inner_blocks = b_mask.shape[0]
    col_blocks = b_mask.shape[1]
    steps = a_mask.shape[1] // inner_blocks
    masked_a = (
        a_blocks.reshape(row_blocks, block, steps * inner_blocks, block)
        * a_mask.astype(jnp.float32)[:, None, :, None]
    ).reshape(rows, steps, inner_blocks * block)
    current = (
        b_panel.reshape(inner_blocks, block, col_blocks, block)
        * b_mask.astype(jnp.float32)[:, None, :, None]
    ).reshape(inner_blocks * block, col_blocks * block)
    total = jnp.zeros((rows, col_blocks * block), jnp.float32)
    for step in range(steps):
        total = total + jnp.dot(
            masked_a[:, step, :],
            current,
            precision=lax.Precision.HIGHEST,
            preferred_element_type=jnp.float32,
        )
        if step + 1 < steps:
            current = from_behind(current, "row", 1)
    return total


def tile(ref, row, col, block):
    return ref.at[
        pl.ds(pl.multiple_of(row * block, block), block),
        pl.ds(pl.multiple_of(col * block, block), block),
    ]


def pack_kernel(mask_ref, b_ref, packed_ref, table_ref, sem):
    inner, cols = mask_ref.shape
    block = packed_ref.shape[1]

    def visit(place, found):
        k, j = place // cols, lax.rem(place, cols)
        used = mask_ref[k, j] != 0
        keep = used & (found < SLOTS)
        table_ref[k, j] = jnp.where(keep, found, -1)

        @pl.when(keep)
        def _():
            pltpu.make_async_copy(
                tile(b_ref, k, j, block), packed_ref.at[found], sem
            ).start()

        return found + keep.astype(jnp.int32)

    found = lax.fori_loop(0, inner * cols, visit, jnp.int32(0))

    @pl.loop(0, found)
    def _(_):
        pltpu.make_async_copy(
            tile(b_ref, 0, 0, block), packed_ref.at[0], sem
        ).wait()


def pack(b_mask, b_panel, block):
    return pl.pallas_call(
        pack_kernel,
        out_shape=(
            jax.ShapeDtypeStruct((SLOTS, block, block), jnp.float32),
            jax.ShapeDtypeStruct(TABLE, jnp.int32),
        ),
        in_specs=[
            pl.BlockSpec(memory_space=pltpu.SMEM),
            pl.BlockSpec(memory_space=pl.ANY),
        ],
        out_specs=(
            pl.BlockSpec(memory_space=pl.ANY),
            pl.BlockSpec(memory_space=pltpu.SMEM),
        ),
        scratch_shapes=[pltpu.SemaphoreType.DMA],
        name="pack",
    )(b_mask, b_panel)


def exchange_kernel(n, packed_ref, table_ref, got_ref, tables_ref, send, recv):
    me = lax.axis_index("row")
    pieces = SLOTS // PIECE
    first = lax.rem(me, 2) == 0

    def at(shift):
        return {"row": lax.rem(me + shift + n, n)}

    def copy(source, step, piece, kind, shift):
        if piece == pieces:
            src = table_ref if source is None else tables_ref.at[source]
            dst = tables_ref.at[step]
        else:
            part = pl.ds(piece * PIECE, PIECE)
            src = packed_ref.at[part] if source is None else got_ref.at[source, part]
            dst = got_ref.at[step, part]
        return pltpu.make_async_remote_copy(
            src_ref=src,
            dst_ref=dst,
            send_sem=send.at[kind, piece],
            recv_sem=recv.at[step, piece],
            device_id=at(shift),
            device_id_type=pl.DeviceIdType.MESH,
        )

    barrier = pltpu.get_barrier_semaphore()

    def greet(shifts):
        for shift in shifts:
            pl.semaphore_signal(
                barrier, inc=1, device_id=at(shift), device_id_type=pl.DeviceIdType.MESH
            )

    order = [pieces] + list(range(pieces))

    def run(senders, targets, sends, forward):
        greet(senders)
        pl.semaphore_wait(barrier, targets)
        started = []
        for piece in order:
            for kind, (step, shift) in enumerate(sends):
                c = copy(None, step, piece, kind, shift)
                c.start()
                started.append(c)
        step, shift = forward
        for piece in order:
            copy(None, 1, piece, 0, 1).wait_recv()
            c = copy(1, step, piece, 2, shift)
            c.start()
            started.append(c)
        for piece in order:
            copy(None, 0, piece, 0, 1).wait_recv()
            copy(None, 2, piece, 0, 1).wait_recv()
        for c in started:
            c.wait_send()

    @pl.when(first)
    def _():
        run((1, -2, -3), 2, ((1, 2), (0, 1)), (2, 1))

    @pl.when(jnp.logical_not(first))
    def _():
        run((-1, -2), 3, ((1, 2), (2, 3)), (0, -1))


def exchange(packed, table):
    n = lax.axis_size("row")
    pieces = SLOTS // PIECE
    return pl.pallas_call(
        functools.partial(exchange_kernel, n),
        out_shape=(
            jax.ShapeDtypeStruct((AHEAD,) + packed.shape, packed.dtype),
            jax.ShapeDtypeStruct((AHEAD,) + table.shape, table.dtype),
        ),
        in_specs=[pl.BlockSpec(memory_space=pl.ANY)] * 2,
        out_specs=(pl.BlockSpec(memory_space=pl.ANY),) * 2,
        scratch_shapes=[
            pltpu.SemaphoreType.DMA((3, pieces + 1)),
            pltpu.SemaphoreType.DMA((3, pieces + 1)),
        ],
        compiler_params=pltpu.CompilerParams(collective_id=0, has_side_effects=True),
        name="exchange",
    )(packed, table)


def multiply_kernel(
    a_mask_ref, own_table, tables_ref, a_ref, packed_ref, got_ref, c_ref,
    a_v, b_v, c_v, a_sem, b_sem, c_sem,
):
    row_blocks, inner = a_mask_ref.shape
    block = b_v.shape[-1]
    cols = c_v.shape[1] // block
    steps = b_v.shape[0]
    per_step = inner // steps

    def fetch(i, k):
        return pltpu.make_async_copy(
            tile(a_ref, i, k, block), tile(a_v, i, k, block), a_sem.at[i]
        )

    loads = [pltpu.make_async_copy(packed_ref, b_v.at[0], b_sem.at[0])]
    for step in range(1, steps):
        loads.append(
            pltpu.make_async_copy(got_ref.at[step - 1], b_v.at[step], b_sem.at[step])
        )
    for load in loads:
        load.start()

    for i in range(row_blocks):
        @pl.loop(0, inner)
        def _(k):
            @pl.when(a_mask_ref[i, k] != 0)
            def _():
                fetch(i, k).start()

    @pl.loop(0, row_blocks * block // 8)
    def _(r):
        c_v[pl.ds(pl.multiple_of(r * 8, 8), 8), :] = jnp.zeros(
            (8, c_v.shape[1]), jnp.float32
        )

    for load in loads:
        load.wait()

    stores = []
    for i in range(row_blocks):
        @pl.loop(0, inner)
        def _(k):
            @pl.when(a_mask_ref[i, k] != 0)
            def _():
                fetch(i, k).wait()

        for step in range(steps):
            @pl.loop(0, per_step)
            def _(kb):
                k = step * per_step + kb

                @pl.when(a_mask_ref[i, k] != 0)
                def _():
                    @pl.loop(0, cols)
                    def _(j):
                        if step == 0:
                            slot = own_table[kb, j]
                        else:
                            slot = tables_ref[step - 1, kb, j]

                        @pl.when(slot >= 0)
                        def _():
                            at = (
                                pl.ds(i * block, block),
                                pl.ds(pl.multiple_of(j * block, block), block),
                            )
                            left = a_v[
                                pl.ds(i * block, block),
                                pl.ds(pl.multiple_of(k * block, block), block),
                            ]
                            c_v[at] += jnp.dot(
                                left,
                                b_v[step, slot],
                                precision=lax.Precision.HIGHEST,
                                preferred_element_type=jnp.float32,
                            )

        band = pl.ds(i * block, block)
        store = pltpu.make_async_copy(c_v.at[band], c_ref.at[band], c_sem.at[i])
        store.start()
        stores.append(store)
    for store in stores:
        store.wait()


def multiply(a_mask, own_table, tables, a_blocks, packed, got, cols):
    rows, width = a_blocks.shape
    block = packed.shape[-1]
    steps = AHEAD + 1
    return pl.pallas_call(
        multiply_kernel,
        out_shape=jax.ShapeDtypeStruct((rows, cols * block), jnp.float32),
        in_specs=[pl.BlockSpec(memory_space=pltpu.SMEM)] * 3
        + [pl.BlockSpec(memory_space=pl.ANY)] * 3,
        out_specs=pl.BlockSpec(memory_space=pl.ANY),
        scratch_shapes=[
            pltpu.VMEM((rows, width), jnp.float32),
            pltpu.VMEM((steps, SLOTS, block, block), jnp.float32),
            pltpu.VMEM((rows, cols * block), jnp.float32),
            pltpu.SemaphoreType.DMA((rows // block,)),
            pltpu.SemaphoreType.DMA((steps,)),
            pltpu.SemaphoreType.DMA((rows // block,)),
        ],
        compiler_params=pltpu.CompilerParams(vmem_limit_bytes=24 * MIB),
        name="multiply",
    )(a_mask, own_table, tables, a_blocks, packed, got)


def shards(a_blocks, a_mask, b_panel, b_mask):
    block = a_blocks.shape[0] // a_mask.shape[0]
    most = lax.pmax(jnp.sum(b_mask), ("groups", "row"))
    packed, table = pack(b_mask, b_panel, block)
    got, tables = exchange(packed, table)
    return lax.cond(
        most <= SLOTS,
        lambda: multiply(a_mask, table, tables, a_blocks, packed, got, b_mask.shape[1]),
        lambda: dense(a_blocks, a_mask, b_panel, b_mask),
    )


def solution(mesh):
    return jax.shard_map(
        shards,
        mesh=mesh,
        in_specs=(
            P(("groups", "row"), None),
            P(("groups", "row"), None),
            P(("groups", "row"), None),
            P(("groups", "row"), None),
        ),
        out_specs=P(("groups", "row"), None),
        check_vma=False,
    )
```

time: 173 us -> 97.9 us (0.57)
  the two profiles are of different devices: /device:TPU:0 before, /device:TPU:4 now
where the time goes in v1:
time: 97.9 us; the launch traced here: 97 us
  Pallas kernels  50.9 us (52%)
  blocking collectives  41.7 us (43%)
  local copies, waits for them, and re-layouts  2.02 us (2%)
  other arithmetic  1.39 us (1%)
    pmax x1, blocking collectives, shards(): most = lax.pmax(jnp.sum(b_mask), ('groups', 'row'))  41.7 us
    pallas_call x1, Pallas kernels, exchange(): pl.pallas_call(functools.partial(exchange_kernel, n), out_shape=(jax.Shap...  38.8 us
    pallas_call x1, Pallas kernels, multiply(): pl.pallas_call(multiply_kernel, out_shape=jax.ShapeDtypeStruct((rows, col...  9.02 us
    pallas_call x1, Pallas kernels, pack(): pl.pallas_call(pack_kernel, out_shape=(jax.ShapeDtypeStruct((SLOTS, block...  3.1 us
    unnamed x6, local copies, waits for them, and re-layouts  2.02 us

profile of v1, /device:TPU:4, one launch (start us, length us, event | category | flops | bytes accessed | tf_op | source)
XLA Modules:
  0.0 97.0 jit_solution(15645994848735303429)
XLA Ops:
  0.0 0.0 copy-start.6
  0.0 0.0 copy-start.7
  0.0 1.4 %reduce_sum.9 = s32[]{:T(128)} reduce(s32[4,16]{1,0:T(4,128)} %mask_ref.1, s32[]{:T(128)} %constant.0.clone.1), dimensions={0,1}, to_apply=%region_0.0 | reduce | flops 63 | bytes 264 | tf_op jit(solution)/shard_map/reduce_sum | solution.py:301
  1.4 41.7 %pmax.7 = s32[]{:T(128)} all-reduce(s32[]{:T(128)} %reduce_sum.9), channel_id=1, replica_groups=mesh['groups'=2,'row'=16] {'groups','row'}, use_global_device_ids=true, to_apply=%region_1.0 | all-reduce | flops 1 | bytes 8 | tf_op jit(solution)/shard_map/pmax | solution.py:301
  43.7 3.1 %pack.1 = (f32[16,128,128]{2,1,0:T(8,128)S(1)}, s32[8,128]{1,0:T(8,128)S(1)}) custom-call(s32[4,16]{1,0:T(4,128)} %mask_ref.1, f32[512,2048]{1,0:T(8,128)} %b_ref.1), custom_call_target="tpu_custom_call" | custom-call | tf_op jit(solution)/shard_map/pack/pallas_call | solution.py:86
  46.8 38.8 %exchange.1 = (f32[3,16,128,128]{3,2,1,0:T(8,128)}, s32[3,8,128]{2,1,0:T(8,128)S(1)}) custom-call(f32[16,128,128]{2,1,0:T(8,128)S(1)} %get-tuple-element.43.packed_ref, s32[8,128]{1,0:T(8,128)S(1)} %get-tuple-element.42.table_ref), custom_call_target="tpu_custom_call" | custom-call | tf_op jit(solution)/shard_map/exchange/pallas_call | solution.py:173
  85.7 0.0 copy-done.6
  85.7 0.0 copy-done.7
  85.7 9.3 %conditional.1 = (f32[512,2048]{1,0:T(8,128)S(1)}) conditional(s32[]{:T(128)} %convert_element_type.9, (f32[512,2048]{1,0:T(8,128)}, s32[4,16]{1,0:T(4,128)S(1)}, s32[4,16]{1,0:T(4,128)S(1)}, f32[512,2048]{1,0:T(8,128)}) %tuple.22, (s32[4,16]{1,0:T(4,128)S(1)}, s32[8,128]{1,0:T(8,128)S(1)}, s32[3,8,128]{2,1,0:T(8,128)S(1)}, f32[512,2048]{1,0:T(8,128)}, ...), branch_computations={%region_2.0_spmd, %region_3.0_spmd} | conditional | flops 25775046656 | bytes 243271424 | solution.py:304
  85.9 9.0 %multiply.1 = f32[512,2048]{1,0:T(8,128)S(1)} custom-call(s32[4,16]{1,0:T(4,128)S(1)} %get-tuple-element.32.a_mask_ref, s32[8,128]{1,0:T(8,128)S(1)} %get-tuple-element.33.own_table, s32[3,8,128]{2,1,0:T(8,128)S(1)} %get-tuple-element.34.tables_ref, f32[512,2048]{1,0:T(8,128)} %get-tuple-element.35.a_ref, f32[16,128,128]{2,1,0:T(8,128)S(1)} %get-tuple-element.36.packed_ref, ...), custom_call_target="tpu_custom_call" | custom-call | tf_op jit(solution)/shard_map/cond/branch_1_fun/multiply/pallas_call | solution.py:280
  94.9 0.0 copy-start.5
  95.0 2.0 %copy-done.5 = f32[512,2048]{1,0:T(8,128)} copy-done((f32[512,2048]{1,0:T(8,128)}, f32[512,2048]{1,0:T(8,128)S(1)}, u32[]{:S(2)}) %copy-start.5) | copy-done | bytes 4194328
Async XLA Ops:
  0.0 85.7 %copy-start.6 = (s32[4,16]{1,0:T(4,128)S(1)}, s32[4,16]{1,0:T(4,128)}, u32[]{:S(2)}) copy-start(s32[4,16]{1,0:T(4,128)} %mask_ref.1) | copy-start | bytes 772
  0.0 85.7 %copy-start.7 = (s32[4,16]{1,0:T(4,128)S(1)}, s32[4,16]{1,0:T(4,128)}, u32[]{:S(2)}) copy-start(s32[4,16]{1,0:T(4,128)} %param.7) | copy-start | bytes 772
  94.9 2.0 %copy-start.5 = (f32[512,2048]{1,0:T(8,128)}, f32[512,2048]{1,0:T(8,128)S(1)}, u32[]{:S(2)}) copy-start(f32[512,2048]{1,0:T(8,128)S(1)} %get-tuple-element.56) | copy-start | bytes 12582916
